TPU v7x, 32 devices: a whole 2x2x4 slice. The times are simulated.
32 devices in a mesh: tower: 2 (over y), narrow: 4 (over z), wide: 4 (over x, core).
Axes of the slice: x: 2, y: 2, z: 4, core: 2. Of those that a mesh axis runs over, the one named last changes fastest.
Arguments:
- features: bfloat16 [4, 8, 256, 2048], P('narrow', ('tower', 'wide')), may hold values from -6 to 6
- w_in: bfloat16 [2048, 4096], P(None, 'narrow'), may hold values from -0.125 to 0.125
- b_in: float32 [4096], P('narrow'), may hold values from -0.5 to 0.5
- w_out: bfloat16 [4096, 256], P('narrow'), may hold values from -0.09375 to 0.09375
- user_emb: bfloat16 [8192, 256], P('narrow'), as said below
- item_ids: int32 [4, 8, 256], P('narrow', ('tower', 'wide')), may hold values from 0 to 8191
Outputs:
- row_loss: float32 [8192], P('narrow')
- item_grad: float32 [4, 8, 256, 256], P('narrow', ('tower', 'wide'))
Inputs may be any that keep to these rules, and one draw needn't show every extreme that they name: `user_emb`: user embeddings.
All inputs are finite; a program needn't handle non-finite values.
Results may differ from a plain program's by a relative error of at most 0.024.
Values may be sent and summed in bfloat16 or wider, within the bound.
A program may use at most 64 MiB of HBM per device.

v0:
```python
import jax
import jax.numpy as jnp
from jax import lax
from jax.sharding import PartitionSpec as P

INV_TEMP = 4.0
EPS = 1e-06
NEG = -1e30


def unit_rows(embed):
    return embed * lax.rsqrt(jnp.sum(embed * embed, axis=1, keepdims=True) + EPS)


def block_scores(user, rid, rglob, vectors, col_ids, col_glob):
    scores = (
        lax.dot_general(user, vectors, (((1,), (1,)), ((), ())), preferred_element_type=jnp.float32)
        * INV_TEMP
    )
    diag = rglob[:, None] == col_glob[None, :]
    keep = (rid[:, None] != col_ids[None, :]) | diag
    return (scores, diag, keep)


def block_scores_cols(vectors, col_ids, col_glob, user, rid, rglob):
    scores = (
        lax.dot_general(vectors, user, (((1,), (1,)), ((), ())), preferred_element_type=jnp.float32)
        * INV_TEMP
    )
    diag = col_glob[:, None] == rglob[None, :]
    keep = (col_ids[:, None] != rid[None, :]) | diag
    return (scores, diag, keep)


def local(features, w_in, b_in, w_out, user_emb, item_ids):
    share = features.shape[2]
    width = features.shape[3]
    embed_width = w_out.shape[1]
    users_dev = user_emb.shape[0]
    groups = lax.axis_size("narrow")
    panel = groups * share
    gathered, gathered_ids = (
        lax.all_gather(features, "narrow", axis=0, tiled=True),
        lax.all_gather(item_ids, "narrow", axis=0, tiled=True),
    )
    rows_in = gathered.reshape(panel, width)
    col_ids = gathered_ids.reshape(panel)
    hidden = jax.nn.relu(jnp.dot(rows_in, w_in, preferred_element_type=jnp.float32) + b_in).astype(
        jnp.bfloat16
    )
    partial_embed = jnp.dot(hidden, w_out, preferred_element_type=jnp.float32)
    item_vec = unit_rows(lax.psum(partial_embed, "narrow")).astype(jnp.bfloat16)
    row_ids = lax.all_gather(item_ids, ("tower", "wide"), axis=1, tiled=True).reshape(users_dev)
    narrow_index = lax.axis_index("narrow")
    panel_index = lax.axis_index(("tower", "wide"))
    row_glob = narrow_index * users_dev + jnp.arange(users_dev, dtype=jnp.int32)
    column = jnp.arange(panel, dtype=jnp.int32)
    col_glob = column // share * users_dev + panel_index * share + column % share
    block = min(512, users_dev)
    count = users_dev // block
    users = user_emb.reshape(count, block, embed_width)
    rid_blocks = row_ids.reshape(count, block)
    rglob_blocks = row_glob.reshape(count, block)

    def local_stats(blk):
        user, rid, rglob = blk
        scores, diag, keep = block_scores(user, rid, rglob, item_vec, col_ids, col_glob)
        masked = jnp.where(keep, scores, NEG)
        top = jnp.max(masked, axis=1)
        mass = jnp.sum(jnp.where(keep, jnp.exp(scores - top[:, None]), 0.0), axis=1)
        pos = jnp.sum(jnp.where(diag, scores, 0.0), axis=1)
        return (top, mass, pos, masked.T)

    def local_stats_only(blk):
        top, mass, pos, masked = local_stats(blk)
        return (top, mass, pos)

    top, mass, pos = lax.map(local_stats_only, (users, rid_blocks, rglob_blocks))
    top = top.reshape(users_dev)
    mass = mass.reshape(users_dev)
    pos = pos.reshape(users_dev)
    global_top = lax.pmax(top, ("tower", "wide"))
    total, global_pos = lax.psum((mass * jnp.exp(top - global_top), pos), ("tower", "wide"))
    lse = global_top + jnp.log(total)
    row_loss = lse - global_pos
    lse_blocks = lse.reshape(count, block)

    def add_block(acc, blk):
        user, rid, rglob, lse_blk = blk
        scores, diag, keep = block_scores_cols(item_vec, col_ids, col_glob, user, rid, rglob)
        coef = (
            jnp.where(keep, jnp.exp(scores - lse_blk[None, :]), 0.0) - diag.astype(jnp.float32)
        ).astype(jnp.bfloat16)
        term = jnp.dot(coef, user, preferred_element_type=jnp.float32)
        return (acc + term, None)

    acc, unused = lax.scan(
        add_block,
        jnp.zeros((share * lax.axis_size("narrow"), embed_width), jnp.float32),
        (users, rid_blocks, rglob_blocks, lse_blocks),
    )
    own_grad = lax.psum_scatter(INV_TEMP * acc, "narrow", scatter_dimension=0, tiled=True)
    return (row_loss, own_grad.reshape(1, 1, share, embed_width))


def solution(mesh):
    return jax.shard_map(
        local,
        mesh=mesh,
        in_specs=(
            P("narrow", ("tower", "wide"), None, None),
            P(None, "narrow"),
            P("narrow"),
            P("narrow", None),
            P("narrow", None),
            P("narrow", ("tower", "wide"), None),
        ),
        out_specs=(P("narrow"), P("narrow", ("tower", "wide"), None, None)),
        check_vma=False,
    )
```

profile of v0, /device:TPU:0, one launch (start us, length us, event | category | flops | bytes accessed | tf_op | source)
XLA Modules:
  0.0 238.5 jit_solution(5663523277225741020)
XLA Ops:
  7.2 0.7 all-gather.2.cloned.1.call-update
  8.0 85.1 %all-gather.2.cloned.1.call-done = bf16[4,1,256,2048]{3,2,1,0:T(8,128)(2,1)} async-done(((bf16[1,1,256,2048]{3,2,1,0:T(8,128)(2,1)}), bf16[4,1,256,2048]{3,2,1,0:T(8,128)(2,1)}) %all-gather.2.cloned.1.call-update) | async-done | bytes 4194320 | tf_op jit(solution)/shard_map/all_gather | solution.py:43
  93.1 9.6 %fusion.48 = f32[1024,256]{1,0:T(8,128)} fusion(bf16[1024,256]{1,0:T(8,128)(2,1)S(1)} %copy-done, f32[1024]{0:T(1024)} %param.12, bf16[1024,2048]{1,0:T(8,128)(2,1)} %bitcast.95, bf16[2048,1024]{1,0:T(8,128)(2,1)} %param.11), kind=kOutput, calls=%fused_computation.64 | convolution fusion | flops 4834983936 | bytes 9965568 | tf_op jit(solution)/shard_map/dot_general | solution.py:51
  102.8 9.0 %all_gather.9 = s32[1,8,256]{2,0,1:T(1,128)S(1)} all-gather(s32[1,1,256]{2,0,1:T(1,128)S(1)} %bitcast.94), channel_id=1, replica_groups=mesh['tower'=2,'narrow'=4,'wide'=4] {'tower','wide'}, dimensions={1}, use_global_device_ids=true | all-gather | bytes 9216 | tf_op jit(solution)/shard_map/all_gather | solution.py:53
  111.9 8.8 %all_gather.10 = s32[4,1,256]{2,1,0:T(1,128)S(1)} all-gather(s32[1,1,256]{2,1,0:T(1,128)S(1)} %copy-done.1), channel_id=1, replica_groups=mesh['tower'=2,'narrow'=4,'wide'=4] {'narrow'}, dimensions={0}, use_global_device_ids=true | all-gather | bytes 5120 | tf_op jit(solution)/shard_map/all_gather | solution.py:44
  120.7 32.6 %all-reduce.3.cloned.1.call-done = f32[1024,256]{1,0:T(8,128)} async-done(((f32[1024,256]{1,0:T(8,128)}), f32[1024,256]{1,0:T(8,128)}) %all-reduce.3.cloned.1.call-update) | async-done | bytes 1048592 | tf_op jit(solution)/shard_map/psum | solution.py:52
  153.3 1.4 multiply_reduce_fusion
  154.8 1.4 multiply_convert_fusion
  156.2 7.8 %while.26 = (s32[]{:T(128)}, f32[4,512]{1,0:T(4,128)S(1)}, f32[4,512]{1,0:T(4,128)S(1)}, f32[4,512]{1,0:T(4,128)S(1)}, s32[4,512]{1,0:T(4,128)S(1)}, /*index=5*/...) while((s32[]{:T(128)}, f32[4,512]{1,0:T(4,128)S(1)}, ...), condition=%wide.region_6.7_spmd.clone, body=%wide.region_2.6_spmd.clone.sunk | while | flops 276313600 | bytes 5038221 | solution.py:78
  156.9 1.1 fusion.70
  158.2 0.7 select_reduce_fusion.3
  158.9 1.1 fusion.70
  160.1 0.7 select_reduce_fusion.3
  160.8 1.1 fusion.70
  162.8 1.1 fusion.70
  164.0 14.1 %pmax.7 = f32[2048]{0:T(1024)S(1)} all-reduce(f32[2048]{0:T(1024)S(1)} %bitcast.84), channel_id=1, replica_groups=mesh['tower'=2,'narrow'=4,'wide'=4] {'tower','wide'}, use_global_device_ids=true, to_apply=%region_7.8 | all-reduce | flops 2048 | bytes 16384 | tf_op jit(solution)/shard_map/pmax | solution.py:82
  178.2 22.3 %all-reduce = (f32[2048]{0:T(1024)S(1)}, f32[2048]{0:T(1024)S(1)}) all-reduce(f32[2048]{0:T(1024)S(1)} %exponential_multiply_fusion, f32[2048]{0:T(1024)S(1)} %bitcast.89), channel_id=1, replica_groups=mesh['tower'=2,'narrow'=4,'wide'=4] {'tower','wide'}, use_global_device_ids=true, to_apply=%region_8.9 | all-reduce | flops 4096 | bytes 32768 | tf_op jit(solution)/shard_map/psum | solution.py:83
  201.1 4.9 %while.27 = (s32[]{:T(128)}, f32[1024,256]{1,0:T(8,128)S(1)}, s32[4,1,256]{2,1,0:T(1,128)S(1)}, s32[4,512]{1,0:T(4,128)S(1)}, s32[4,512]{1,0:T(4,128)S(1)}, /*in...) while((s32[]{:T(128)}, f32[1024,256]{1,0:T(8,128)S(1)}, ...), condition=%wide.region_11.12_spmd.clone, body=%wide.region_10.11_spmd.clone.sunk | while | flops 542129152 | bytes 3177603 | solution.py:97
  201.2 1.2 fusion.75
  202.4 1.2 fusion.75
  203.7 1.2 fusion.75
  204.9 1.2 fusion.75
  206.1 1.1 broadcast_multiply_fusion
  207.2 24.8 %reduce-scatter.2.cloned.1.call-done = f32[256,256]{1,0:T(8,128)} async-done(((f32[1024,256]{1,0:T(8,128)}), f32[256,256]{1,0:T(8,128)}) %reduce-scatter.2.cloned.1.call-update) | async-done | bytes 262160 | tf_op jit(solution)/shard_map/reduce_scatter | solution.py:102
  (59 shorter events, 3.0 us)
Async XLA Ops:
  7.2 85.9 %copy-start = (bf16[1024,256]{1,0:T(8,128)(2,1)S(1)}, bf16[1024,256]{1,0:T(8,128)(2,1)}, u32[]{:S(2)}) copy-start(bf16[1024,256]{1,0:T(8,128)(2,1)} %param.13) | copy-start | bytes 1572868
  7.2 85.9 %all-gather.2.cloned.1.call-start = ((), (), s32[]{:S(2)}) async-start(), calls=%async_computation.1 | async-start | bytes 5242880 | tf_op jit(solution)/shard_map/all_gather | solution.py:43
  7.9 145.4 %all-reduce.3.cloned.1.call-start = ((), (), s32[]{:S(2)}) async-start(), calls=%async_computation.2 | async-start | bytes 2097152 | tf_op jit(solution)/shard_map/psum | solution.py:52
  93.1 9.8 %copy-start.1 = (s32[1,1,256]{2,1,0:T(1,128)S(1)}, s32[1,1,256]{2,1,0:T(1,128)}, u32[]{:S(2)}) copy-start(s32[1,1,256]{2,1,0:T(1,128)} %param.15) | copy-start | bytes 3076
  102.7 53.5 %copy-start.2 = (bf16[2048,256]{1,0:T(8,128)(2,1)S(1)}, bf16[2048,256]{1,0:T(8,128)(2,1)}, u32[]{:S(2)}) copy-start(bf16[2048,256]{1,0:T(8,128)(2,1)} %param.14) | copy-start | bytes 3145732
  102.7 129.3 %reduce-scatter.2.cloned.1.call-start = ((), (), s32[]{:S(2)}) async-start(), calls=%async_computation.3 | async-start | bytes 1310720 | tf_op jit(solution)/shard_map/reduce_scatter | solution.py:102
Sparse Core Ops, SparseCore 0:
  9.6 83.4 all-gather.1
  102.9 50.3 all-reduce.2
  207.3 24.6 reduce-scatter.1
where the time goes:
time: 239 us
  waiting for transfers between devices  143 us (60%)
  blocking collectives  54.2 us (23%)
  matrix products  17 us (7%)
  between operations  13.9 us (6%)
  other arithmetic  8.95 us (4%)
    all_gather x1, waiting for transfers between devices, local(): lax.all_gather(features, 'narrow', axis=0, tiled=True)  85.1 us
    psum x1, waiting for transfers between devices, local(): item_vec = unit_rows(lax.psum(partial_embed, 'narrow')).astype(jnp.bfloat16)  32.6 us
    reduce_scatter x1, waiting for transfers between devices, local(): lax.psum_scatter(INV_TEMP * acc, 'narrow', scatter_dimension=0, tiled=True)  24.8 us
    psum x1, blocking collectives, local(): lax.psum((mass * jnp.exp(top - global_top), pos), ('tower', 'wide'))  22.3 us
    pmax x1, blocking collectives, local(): global_top = lax.pmax(top, ('tower', 'wide'))  14.1 us
    dot_general x1, matrix products, local(): partial_embed = jnp.dot(hidden, w_out, preferred_element_type=jnp.float32)  9.62 us
    all_gather x1, blocking collectives, local(): lax.all_gather(item_ids, ('tower', 'wide'), axis=1, tiled=True)  9.02 us
    all_gather x1, blocking collectives, local(): lax.all_gather(item_ids, 'narrow', axis=0, tiled=True)  8.76 us
  transfers between devices with their start and end apart: 3, of which 3 were waited for; matrix products, arithmetic and copies ran while one was open for 0% of the time, Pallas kernels for 0%

commit v1 on v0

--- a/solution.py
+++ b/solution.py
@@ -80,7 +80,9 @@
     mass = mass.reshape(users_dev)
     pos = pos.reshape(users_dev)
     global_top = lax.pmax(top, ("tower", "wide"))
-    total, global_pos = lax.psum((mass * jnp.exp(top - global_top), pos), ("tower", "wide"))
+    total, global_pos = lax.psum(
+        lax.psum((mass * jnp.exp(top - global_top), pos), axis_name="wide"), axis_name="tower"
+    )
     lse = global_top + jnp.log(total)
     row_loss = lse - global_pos
     lse_blocks = lse.reshape(count, block)

time: 239 us -> 235 us (0.983)
  blocking collectives: 54.2 us -> 49.1 us
    psum x1 -> x2, blocking collectives: 22.3 us -> 17.3 us  [the longest x1 10.1 us: local(): lax.psum((mass * jnp.exp(top - global_top), pos), axis_name='wide')]
where the time goes in v1:
time: 235 us; the launch traced here: 234 us
  waiting for transfers between devices  144 us (61%)
  blocking collectives  49.1 us (21%)
  matrix products  17 us (7%)
  between operations  13.9 us (6%)
  other arithmetic  8.95 us (4%)
    all_gather x1, waiting for transfers between devices, local(): lax.all_gather(features, 'narrow', axis=0, tiled=True)  85.1 us
    psum x1, waiting for transfers between devices, local(): item_vec = unit_rows(lax.psum(partial_embed, 'narrow')).astype(jnp.bfloat16)  32.6 us
    reduce_scatter x1, waiting for transfers between devices, local(): lax.psum_scatter(INV_TEMP * acc, 'narrow', scatter_dimension=0, tiled=True)  25.7 us
    pmax x1, blocking collectives, local(): global_top = lax.pmax(top, ('tower', 'wide'))  14.1 us
    psum x1, blocking collectives, local(): lax.psum((mass * jnp.exp(top - global_top), pos), axis_name='wide')  10.1 us
    dot_general x1, matrix products, local(): partial_embed = jnp.dot(hidden, w_out, preferred_element_type=jnp.float32)  9.62 us
    all_gather x1, blocking collectives, local(): lax.all_gather(item_ids, ('tower', 'wide'), axis=1, tiled=True)  9.02 us
    all_gather x1, blocking collectives, local(): lax.all_gather(item_ids, 'narrow', axis=0, tiled=True)  8.76 us
  transfers between devices with their start and end apart: 3, of which 3 were waited for; matrix products, arithmetic and copies ran while one was open for 0% of the time, Pallas kernels for 0%

profile of v1, /device:TPU:0, one launch (start us, length us, event | category | flops | bytes accessed | tf_op | source)
XLA Modules:
  0.0 234.3 jit_solution(12220538595648621567)
XLA Ops:
  7.2 0.7 all-gather.2.cloned.1.call-update
  8.0 85.1 %all-gather.2.cloned.1.call-done = bf16[4,1,256,2048]{3,2,1,0:T(8,128)(2,1)} async-done(((bf16[1,1,256,2048]{3,2,1,0:T(8,128)(2,1)}), bf16[4,1,256,2048]{3,2,1,0:T(8,128)(2,1)}) %all-gather.2.cloned.1.call-update) | async-done | bytes 4194320 | tf_op jit(solution)/shard_map/all_gather | solution.py:43
  93.1 9.6 %fusion.48 = f32[1024,256]{1,0:T(8,128)} fusion(bf16[1024,256]{1,0:T(8,128)(2,1)S(1)} %copy-done, f32[1024]{0:T(1024)} %param.12, bf16[1024,2048]{1,0:T(8,128)(2,1)} %bitcast.95, bf16[2048,1024]{1,0:T(8,128)(2,1)} %param.11), kind=kOutput, calls=%fused_computation.64 | convolution fusion | flops 4834983936 | bytes 9965568 | tf_op jit(solution)/shard_map/dot_general | solution.py:51
  102.8 9.0 %all_gather.9 = s32[1,8,256]{2,0,1:T(1,128)S(1)} all-gather(s32[1,1,256]{2,0,1:T(1,128)S(1)} %bitcast.94), channel_id=1, replica_groups=mesh['tower'=2,'narrow'=4,'wide'=4] {'tower','wide'}, dimensions={1}, use_global_device_ids=true | all-gather | bytes 9216 | tf_op jit(solution)/shard_map/all_gather | solution.py:53
  111.9 8.8 %all_gather.10 = s32[4,1,256]{2,1,0:T(1,128)S(1)} all-gather(s32[1,1,256]{2,1,0:T(1,128)S(1)} %copy-done.1), channel_id=1, replica_groups=mesh['tower'=2,'narrow'=4,'wide'=4] {'narrow'}, dimensions={0}, use_global_device_ids=true | all-gather | bytes 5120 | tf_op jit(solution)/shard_map/all_gather | solution.py:44
  120.7 32.6 %all-reduce.4.cloned.1.call-done = f32[1024,256]{1,0:T(8,128)} async-done(((f32[1024,256]{1,0:T(8,128)}), f32[1024,256]{1,0:T(8,128)}) %all-reduce.4.cloned.1.call-update) | async-done | bytes 1048592 | tf_op jit(solution)/shard_map/psum | solution.py:52
  153.3 1.4 multiply_reduce_fusion
  154.8 1.4 multiply_convert_fusion
  156.2 7.8 %while.26 = (s32[]{:T(128)}, f32[4,512]{1,0:T(4,128)S(1)}, f32[4,512]{1,0:T(4,128)S(1)}, f32[4,512]{1,0:T(4,128)S(1)}, s32[4,512]{1,0:T(4,128)S(1)}, /*index=5*/...) while((s32[]{:T(128)}, f32[4,512]{1,0:T(4,128)S(1)}, ...), condition=%wide.region_6.7_spmd.clone, body=%wide.region_2.6_spmd.clone.sunk | while | flops 276313600 | bytes 5038221 | solution.py:78
  156.9 1.1 fusion.70
  158.9 1.1 fusion.70
  160.8 1.1 fusion.70
  162.1 0.7 select_reduce_fusion.3
  162.8 1.1 fusion.70
  164.0 14.1 %pmax.7 = f32[2048]{0:T(1024)S(1)} all-reduce(f32[2048]{0:T(1024)S(1)} %bitcast.84), channel_id=1, replica_groups=mesh['tower'=2,'narrow'=4,'wide'=4] {'tower','wide'}, use_global_device_ids=true, to_apply=%region_7.8 | all-reduce | flops 2048 | bytes 16384 | tf_op jit(solution)/shard_map/pmax | solution.py:82
  178.2 10.1 %all-reduce = (f32[2048]{0:T(1024)S(1)}, f32[2048]{0:T(1024)S(1)}) all-reduce(f32[2048]{0:T(1024)S(1)} %exponential_multiply_fusion, f32[2048]{0:T(1024)S(1)} %bitcast.89), channel_id=1, replica_groups=mesh['tower'=2,'narrow'=4,'wide'=4] {'wide'}, use_global_device_ids=true, to_apply=%region_8.9 | all-reduce | flops 4096 | bytes 32768 | tf_op jit(solution)/shard_map/psum | solution.py:84
  188.3 7.1 %all-reduce.1 = (f32[2048]{0:T(1024)S(1)}, f32[2048]{0:T(1024)S(1)}) all-reduce(f32[2048]{0:T(1024)S(1)} %get-tuple-element.203, f32[2048]{0:T(1024)S(1)} %get-tuple-element.204), channel_id=1, replica_groups=mesh['tower'=2,'narrow'=4,'wide'=4] {'tower'}, use_global_device_ids=true, to_apply=%region_9.10 | all-reduce | flops 4096 | bytes 32768 | tf_op jit(solution)/shard_map/psum | solution.py:83
  196.1 4.9 %while.27 = (s32[]{:T(128)}, f32[1024,256]{1,0:T(8,128)S(1)}, s32[4,1,256]{2,1,0:T(1,128)S(1)}, s32[4,512]{1,0:T(4,128)S(1)}, s32[4,512]{1,0:T(4,128)S(1)}, /*in...) while((s32[]{:T(128)}, f32[1024,256]{1,0:T(8,128)S(1)}, ...), condition=%wide.region_13.14_spmd.clone, body=%wide.region_12.13_spmd.clone.sunk | while | flops 542129152 | bytes 3177603 | solution.py:99
  196.1 1.2 fusion.75
  197.3 1.2 fusion.75
  198.6 1.2 fusion.75
  199.8 1.2 fusion.75
  201.0 1.1 broadcast_multiply_fusion
  202.1 25.7 %reduce-scatter.2.cloned.1.call-done = f32[256,256]{1,0:T(8,128)} async-done(((f32[1024,256]{1,0:T(8,128)}), f32[256,256]{1,0:T(8,128)}) %reduce-scatter.2.cloned.1.call-update) | async-done | bytes 262160 | tf_op jit(solution)/shard_map/reduce_scatter | solution.py:104
  (60 shorter events, 3.7 us)
Async XLA Ops:
  7.2 85.9 %copy-start = (bf16[1024,256]{1,0:T(8,128)(2,1)S(1)}, bf16[1024,256]{1,0:T(8,128)(2,1)}, u32[]{:S(2)}) copy-start(bf16[1024,256]{1,0:T(8,128)(2,1)} %param.13) | copy-start | bytes 1572868
  7.2 85.9 %all-gather.2.cloned.1.call-start = ((), (), s32[]{:S(2)}) async-start(), calls=%async_computation.1 | async-start | bytes 5242880 | tf_op jit(solution)/shard_map/all_gather | solution.py:43
  7.9 145.4 %all-reduce.4.cloned.1.call-start = ((), (), s32[]{:S(2)}) async-start(), calls=%async_computation.2 | async-start | bytes 2097152 | tf_op jit(solution)/shard_map/psum | solution.py:52
  93.1 9.8 %copy-start.1 = (s32[1,1,256]{2,1,0:T(1,128)S(1)}, s32[1,1,256]{2,1,0:T(1,128)}, u32[]{:S(2)}) copy-start(s32[1,1,256]{2,1,0:T(1,128)} %param.15) | copy-start | bytes 3076
  102.7 53.5 %copy-start.2 = (bf16[2048,256]{1,0:T(8,128)(2,1)S(1)}, bf16[2048,256]{1,0:T(8,128)(2,1)}, u32[]{:S(2)}) copy-start(bf16[2048,256]{1,0:T(8,128)(2,1)} %param.14) | copy-start | bytes 3145732
  102.7 125.1 %reduce-scatter.2.cloned.1.call-start = ((), (), s32[]{:S(2)}) async-start(), calls=%async_computation.3 | async-start | bytes 1310720 | tf_op jit(solution)/shard_map/reduce_scatter | solution.py:104
Sparse Core Ops, SparseCore 0:
  9.6 83.4 all-gather.1
  102.9 50.3 all-reduce.3
  202.2 25.5 reduce-scatter.1
